TPU v7x, 32 devices: a whole 2x2x4 slice. The times are simulated.
32 devices in a mesh: groups: 2 (over x), tensor: 16 (over z, y, core).
Axes of the slice: x: 2, y: 2, z: 4, core: 2. Of those that a mesh axis runs over, the one named last changes fastest.
Arguments:
- tokens: bfloat16 [256, 8192], P(('groups', 'tensor')), parts along dimension 0, may hold values from -6 to 6
- gate_weight: bfloat16 [8192, 28672], P(None, 'tensor'), may hold values from -0.0625 to 0.0625
- up_weight: bfloat16 [8192, 28672], P(None, 'tensor'), may hold values from -0.0625 to 0.0625
- first_store: bfloat16 [64, 16, 32, 512], P(('groups', 'tensor')), parts along dimension 0, may hold values from -0.0625 to 0.0625
- second_store: bfloat16 [64, 16, 32, 1792], P(('groups', 'tensor')), parts along dimension 0, may hold values from -1.5 to 1.5
- adapter_ids: int32 [2], P('groups'), parts along dimension 0, may hold values from 0 to 31
- owner_map: int32 [64], P('groups'), parts along dimension 0, may hold values from 0 to 31, each once
Outputs:
- hidden: bfloat16 [256, 28672], P('groups', 'tensor'), parts along dimension 0
There are 2 independent parts, one for each index of `groups`. A program takes and returns all parts, laid end to end along the dimension named above; an argument that names none is the same for every part. Nothing has to cross between parts.
Inputs may be any that keep to these rules, and one draw needn't show every extreme that they name: `adapter_ids`: prompt p covers tokens p * 128 to (p + 1) * 128 - 1. `owner_map`: A permutation of the slots: slot s is entry s % 2 of the store of index s // 2 of tensor.
All inputs are finite; a program needn't handle non-finite values.
Results may differ from a plain program's by a relative error of at most 0.0051.
Values may be sent and summed in bfloat16 or wider, within the bound.
A program may use at most 192 MiB of HBM per device.

v0:
```python
import jax
import jax.numpy as jnp
from jax import lax
from jax.sharding import PartitionSpec as P

PLEN = 128


def spread(value, axis, root):
    mine = lax.axis_index(axis) == root
    return lax.psum(jnp.where(mine, value, jnp.zeros_like(value)), axis)


def per_device(tokens, gate_weight, up_weight, first_store, second_store, adapter_ids, owner_map):
    own_index = lax.axis_index("tensor")
    tok_dev = tokens.shape[0]
    prompts = adapter_ids.shape[0]
    keep_count = first_store.shape[0]
    doubled = second_store.shape[2]
    rank = doubled // 2
    width = gate_weight.shape[1]
    matches = adapter_ids[:, None] == jnp.arange(owner_map.shape[0], dtype=jnp.int32)[None, :]
    slots = jnp.sum(jnp.where(matches, owner_map[None, :], 0), axis=1)
    own_prompt = own_index * tok_dev // PLEN

    def fetch_step(prompt, held):
        slot = lax.dynamic_index_in_dim(slots, prompt, 0, keepdims=False)
        piece = lax.dynamic_index_in_dim(first_store, slot % keep_count, 0, keepdims=False)
        landed = spread(piece, "tensor", slot // keep_count)
        return jnp.where(prompt == own_prompt, landed, held)

    blocked = lax.fori_loop(0, prompts, fetch_step, jnp.zeros(first_store.shape[1:], jnp.bfloat16))
    factor = jnp.transpose(blocked, (1, 0, 2)).reshape(doubled, tokens.shape[1])
    lowrank = jnp.dot(tokens, factor.T, preferred_element_type=jnp.float32).astype(jnp.bfloat16)
    whole, low_all = (
        lax.all_gather(tokens, "tensor", axis=0, tiled=True),
        lax.all_gather(lowrank, "tensor", axis=0, tiled=True),
    )
    spread_second = lax.all_to_all(second_store, "tensor", split_axis=1, concat_axis=0, tiled=True)
    spread_second = spread_second.reshape(spread_second.shape[0], 2, rank, width)
    picked_second = jnp.take(spread_second, slots, axis=0)
    low_four = low_all.reshape(prompts, PLEN, 2, rank)
    delta = jnp.einsum(
        "ptgr,pgrf->gptf", low_four, picked_second, preferred_element_type=jnp.float32
    )
    delta = delta.reshape(2, prompts * PLEN, width)
    gate = jnp.dot(whole, gate_weight, preferred_element_type=jnp.float32) + delta[0]
    lifted = jnp.dot(whole, up_weight, preferred_element_type=jnp.float32) + delta[1]
    return (jax.nn.silu(gate) * lifted).astype(jnp.bfloat16)


def solution(mesh):
    placed = (
        P(("groups", "tensor"), None),
        P(None, "tensor"),
        P(None, "tensor"),
        P(("groups", "tensor"), None, None, None),
        P(("groups", "tensor"), None, None, None),
        P("groups"),
        P("groups"),
    )
    return jax.shard_map(
        per_device, mesh=mesh, in_specs=placed, out_specs=P("groups", "tensor"), check_vma=False
    )
```

profile of v0, /device:TPU:0, one launch (start us, length us, event | category | flops | bytes accessed | tf_op | source)
XLA Modules:
  0.0 238.7 jit_solution(15207574215422660599)
XLA Ops:
  6.5 4.2 %copy.15 = bf16[2,16,32,1792]{3,2,0,1:T(8,128)(2,1)} copy(bf16[2,16,32,1792]{3,2,1,0:T(8,128)(2,1)} %param.11) | data formatting | bytes 7340032 | tf_op args[4]
  10.7 0.0 copy-start.3
  10.7 0.0 copy-start.2
  10.7 7.6 %all-to-all-start = ((bf16[2,16,32,1792]{3,2,0,1:T(8,128)(2,1)}), bf16[2,16,32,1792]{3,2,0,1:T(8,128)(2,1)}, u32[]{:S(2)}, u32[]{:S(2)}) async-start(bf16[2,16,32,1792]{3,2,0,1:T(8,128)(2,1)} %copy.15), calls=%async_computation | async-start | bytes 7340032 | tf_op jit(solution)/shard_map/all_to_all | solution.py:39
  18.3 0.0 copy-start.1
  18.3 0.0 all-reduce.2.cloned.1.call-start
  19.0 0.0 copy-done.3
  19.0 0.6 fusion.7
  21.9 0.0 copy-done.2
  22.0 0.8 select_bitcast_fusion.1
  22.8 0.0 all-reduce.2.cloned.1.call-update
  22.8 0.0 all-gather.2.cloned.1.call-start
  22.9 0.7 all-gather.2.cloned.1.call-update
  25.2 133.4 %all-reduce.2.cloned.1.call-done = bf16[16,32,512]{2,1,0:T(8,128)(2,1)} async-done(((bf16[16,32,512]{2,1,0:T(8,128)(2,1)}), bf16[16,32,512]{2,1,0:T(8,128)(2,1)}) %all-reduce.2.cloned.1.call-update) | async-done | bytes 524304 | tf_op jit(solution)/shard_map/while/body/eval_jaxpr/psum | solution.py:11
  158.7 1.1 select_bitcast_fusion
  159.8 0.0 copy-done.1
  159.8 0.2 fusion.2
  160.0 21.0 %all_gather.7 = bf16[128,32]{1,0:T(8,128)(2,1)S(1)} all-gather(bf16[8,32]{1,0:T(8,128)(2,1)S(1)} %fusion.2), channel_id=1, replica_groups=mesh['groups'=2,'tensor'=16] {'tensor'}, dimensions={0}, use_global_device_ids=true | all-gather | bytes 8704 | tf_op jit(solution)/shard_map/all_gather | solution.py:37
  181.0 0.1 copy.14
  181.1 0.0 all-to-all-done
  181.1 1.3 fusion.3
  182.5 20.3 %all-gather.2.cloned.1.call-done = bf16[128,8192]{1,0:T(8,128)(2,1)} async-done(((bf16[8,8192]{1,0:T(8,128)(2,1)}), bf16[128,8192]{1,0:T(8,128)(2,1)}) %all-gather.2.cloned.1.call-update) | async-done | bytes 2097168 | tf_op jit(solution)/shard_map/all_gather | solution.py:36
  202.8 0.0 copy-start
  202.8 14.8 %convolution_add_fusion.1 = f32[128,1792]{1,0:T(8,128)S(1)} fusion(bf16[128,8192]{1,0:T(8,128)(2,1)} %all-gather.2.cloned.1.call-done, bf16[8192,1792]{1,0:T(8,128)(2,1)} %param.8, f32[2,128,1792]{2,1,0:T(8,128)S(1)} %fusion.3), kind=kOutput, calls=%fused_computation.2 | convolution fusion | flops 3758325760 | bytes 33292288 | tf_op jit(solution)/shard_map/dot_general | solution.py:47
  217.6 0.0 copy-done
  217.6 14.3 %fusion.1 = bf16[128,1792]{1,0:T(8,128)(2,1)} fusion(bf16[128,8192]{1,0:T(8,128)(2,1)S(1)} %copy-done, bf16[8192,1792]{1,0:T(8,128)(2,1)} %param.9, f32[2,128,1792]{2,1,0:T(8,128)S(1)} %fusion.3, f32[128,1792]{1,0:T(8,128)S(1)} %convolution_add_fusion.1), kind=kOutput, calls=%fused_computation.3 | convolution fusion | flops 3759702016 | bytes 33751040 | tf_op jit(solution)/shard_map/dot_general | solution.py:48
  (1 shorter events, 0.0 us)
Async XLA Ops:
  10.7 8.3 %copy-start.3 = (s32[32]{0:T(128)S(1)}, s32[32]{0:T(128)}, u32[]{:S(2)}) copy-start(s32[32]{0:T(128)} %param.13) | copy-start | bytes 388
  10.7 11.2 %copy-start.2 = (bf16[2,16,32,512]{3,2,1,0:T(8,128)(2,1)S(1)}, bf16[2,16,32,512]{3,2,1,0:T(8,128)(2,1)}, u32[]{:S(2)}) copy-start(bf16[2,16,32,512]{3,2,1,0:T(8,128)(2,1)} %param.10) | copy-start | bytes 3145732
  10.7 170.4 %all-to-all-start = ((bf16[2,16,32,1792]{3,2,0,1:T(8,128)(2,1)}), bf16[2,16,32,1792]{3,2,0,1:T(8,128)(2,1)}, u32[]{:S(2)}, u32[]{:S(2)}) async-start(bf16[2,16,32,1792]{3,2,0,1:T(8,128)(2,1)} %copy.15), calls=%async_computation | async-start | bytes 7340032 | tf_op jit(solution)/shard_map/all_to_all | solution.py:39
  18.3 141.5 %copy-start.1 = (bf16[8,8192]{1,0:T(8,128)(2,1)S(1)}, bf16[8,8192]{1,0:T(8,128)(2,1)}, u32[]{:S(2)}) copy-start(bf16[8,8192]{1,0:T(8,128)(2,1)} %param.7) | copy-start | bytes 393220
  18.3 140.3 %all-reduce.2.cloned.1.call-start = ((), (), s32[]{:S(2)}) async-start(), calls=%async_computation.2 | async-start | bytes 1048576 | tf_op jit(solution)/shard_map/while/body/eval_jaxpr/psum | solution.py:11
  22.8 180.0 %all-gather.2.cloned.1.call-start = ((), (), s32[]{:S(2)}) async-start(), calls=%async_computation.1 | async-start | bytes 2228224 | tf_op jit(solution)/shard_map/all_gather | solution.py:36
  202.8 14.8 %copy-start = (bf16[128,8192]{1,0:T(8,128)(2,1)S(1)}, bf16[128,8192]{1,0:T(8,128)(2,1)}, u32[]{:S(2)}) copy-start(bf16[128,8192]{1,0:T(8,128)(2,1)} %all-gather.2.cloned.1.call-done) | copy-start | bytes 6291460
Sparse Core Ops, SparseCore 0:
  22.9 135.6 all-reduce.1
  160.8 41.9 all-gather.1
where the time goes:
time: 239 us
  waiting for transfers between devices  154 us (64%)
  matrix products  30.6 us (13%)
  blocking collectives  21 us (9%)
  between operations  18.1 us (8%)
  starting transfers between devices  7.64 us (3%)
  local copies, waits for them, and re-layouts  4.34 us (2%)
  other arithmetic  2.53 us (1%)
    psum x1, waiting for transfers between devices, spread(): return lax.psum(jnp.where(mine, value, jnp.zeros_like(value)), axis)  133 us
    all_gather x1, blocking collectives, per_device(): lax.all_gather(lowrank, 'tensor', axis=0, tiled=True)  21 us
    all_gather x1, waiting for transfers between devices, per_device(): lax.all_gather(tokens, 'tensor', axis=0, tiled=True)  20.3 us
    dot_general x1, matrix products, per_device(): jnp.dot(whole, gate_weight, preferred_element_type=jnp.float32) + delta[0]  14.8 us
    dot_general x1, matrix products, per_device(): jnp.dot(whole, up_weight, preferred_element_type=jnp.float32) + delta[1]  14.3 us
    all_to_all x1, starting transfers between devices, per_device(): lax.all_to_all(second_store, 'tensor', split_axis=1, concat_axis=0, tiled...  7.56 us
  transfers between devices with their start and end apart: 3, of which 2 were waited for; matrix products, arithmetic and copies ran while one was open for 2% of the time, Pallas kernels for 0%

commit v1 on v0

--- a/solution.py
+++ b/solution.py
@@ -1,9 +1,16 @@
+import functools
 import jax
 import jax.numpy as jnp
 from jax import lax
+from jax.experimental import pallas as pl
+from jax.experimental.pallas import tpu as pltpu
 from jax.sharding import PartitionSpec as P
 
 PLEN = 128
+CHUNKS = 8
+SLOTS = 12
+R1_AT, R2_AT = 4, 9
+MESH = pl.DeviceIdType.MESH
 
 
 def spread(value, axis, root):
@@ -11,7 +18,7 @@
     return lax.psum(jnp.where(mine, value, jnp.zeros_like(value)), axis)
 
 
-def per_device(tokens, gate_weight, up_weight, first_store, second_store, adapter_ids, owner_map):
+def general(tokens, gate_weight, up_weight, first_store, second_store, adapter_ids, owner_map):
     own_index = lax.axis_index("tensor")
     tok_dev = tokens.shape[0]
     prompts = adapter_ids.shape[0]
@@ -49,7 +56,312 @@
     return (jax.nn.silu(gate) * lifted).astype(jnp.bfloat16)
 
 
+def kernel(
+    nz, keep,
+    tok, wg, wu, f1, ss, ids, omap, out,
+    x, xf, w, ag, au, pbuf, sbuf, qbuf, tbuf, fbuf, lacc, lstage, lc, ly, lz,
+    s_tok, s_w, s_p, zs, zr, ys, yr, cs, cr, ps, pr, rys, ryr, rzs, rzr, ls, lr,
+):
+    me = lax.axis_index("tensor")
+    core = lax.rem(me, 2)
+    yy = lax.rem(me // 2, 2)
+    zz = me // 4
+    kc = xf.shape[2]
+    width = wg.shape[1]
+    sub = kc // f1.shape[3]
+    nw = 2 * CHUNKS
+
+    def at(z, y, c):
+        return {"tensor": z * 4 + y * 2 + c}
+
+    def far(d):
+        return lax.rem(zz + d, nz)
+
+    def near(d):
+        return lax.rem(zz + nz - d, nz)
+
+    def remote(src, dst, send, recv, dev):
+        return pltpu.make_async_remote_copy(
+            src_ref=src, dst_ref=dst, send_sem=send, recv_sem=recv,
+            device_id=dev, device_id_type=MESH,
+        )
+
+    def w_copy(src, chunk, half):
+        slot = lax.rem(chunk * 2 + half, SLOTS)
+        rows = pl.ds(pl.multiple_of(chunk * kc, kc), kc)
+        return pltpu.make_async_copy(src.at[rows, :], w.at[slot], s_w.at[slot])
+
+    partners = [at(zz, yy, 1 - core), at(zz, 1 - yy, core)]
+    partners += [at(far(d), yy, core) for d in range(1, nz)]
+    barrier = pltpu.get_barrier_semaphore()
+    for dev in partners:
+        pl.semaphore_signal(barrier, inc=1, device_id=dev, device_id_type=MESH)
+
+    def cols(ch):
+        return pl.ds(pl.multiple_of(ch * kc, kc), kc)
+
+    def own_copy(ch):
+        return pltpu.make_async_copy(
+            tok.at[:, cols(ch)], x.at[ch, core, yy, zz], s_tok.at[ch]
+        )
+
+    def z_copy(ch, d):
+        return remote(
+            tok.at[:, cols(ch)], x.at[ch, core, yy, zz],
+            zs.at[ch, d - 1], zr.at[ch, d - 1], at(far(d), yy, core),
+        )
+
+    def z_wait(ch, d):
+        remote(
+            tok.at[:, cols(ch)], x.at[ch, core, yy, near(d)],
+            zs.at[ch, d - 1], zr.at[ch, d - 1], at(far(d), yy, core),
+        ).wait_recv()
+
+    def y_copy(ch, side):
+        part = x.at[ch, core, side]
+        return remote(part, part, ys.at[ch], yr.at[ch], at(zz, 1 - yy, core))
+
+    def c_copy(ch, side):
+        part = x.at[ch, side]
+        return remote(part, part, cs.at[ch], cr.at[ch], at(zz, yy, 1 - core))
+
+    own_p = pltpu.make_async_copy(ss.at[:, :, :, core], pbuf.at[pl.ds(0, keep)], s_p.at[0])
+    far_p = remote(
+        ss.at[:, :, :, 1 - core], pbuf.at[pl.ds(keep, keep)], ps.at[0], pr.at[0],
+        at(zz, yy, 1 - core),
+    )
+
+    def ry_copy(z):
+        return remote(
+            sbuf.at[z], qbuf.at[yy, z], rys.at[z], ryr.at[z], at(zz, 1 - yy, core)
+        )
+
+    def rz_copy(d):
+        return remote(
+            tbuf.at[far(d)], fbuf.at[zz], rzs.at[d - 1], rzr.at[d - 1], at(far(d), yy, core)
+        )
+
+    def l_copy(hop, src, dst, dev):
+        return remote(src, dst, ls.at[hop], lr.at[hop], dev)
+
+    l_core = l_copy(0, lc.at[core], lc.at[core], at(zz, yy, 1 - core))
+    l_y = l_copy(1, ly.at[yy], ly.at[yy], at(zz, 1 - yy, core))
+
+    def l_z(d):
+        return l_copy(1 + d, lz.at[zz], lz.at[zz], at(far(d), yy, core))
+
+    def own_loop(ch, _):
+        own_copy(ch).start()
+        return 0
+
+    lax.fori_loop(0, CHUNKS, own_loop, 0)
+    for j in range(SLOTS // 2):
+        w_copy(wg, j, 0).start()
+        w_copy(wu, j, 1).start()
+    own_p.start()
+    slot = omap[ids[0]]
+    kslot = lax.rem(slot, keep)
+    owner = slot // keep
+    oc = lax.rem(owner, 2)
+    oy = lax.rem(owner // 2, 2)
+    oz = owner // 4
+    pick = jnp.where(oc == core, 0, keep) + kslot
+    ag[...] = jnp.zeros_like(ag)
+    au[...] = jnp.zeros_like(au)
+    lacc[...] = jnp.zeros_like(lacc)
+    pl.semaphore_wait(barrier, len(partners))
+
+    def z_loop(ch, _):
+        for d in range(1, nz):
+            z_copy(ch, d).start()
+        return 0
+
+    lax.fori_loop(0, CHUNKS, z_loop, 0)
+    far_p.start()
+
+    def step(i, _):
+        @pl.when(i < CHUNKS)
+        def _():
+            own_copy(i).wait()
+            for d in range(1, nz):
+                z_wait(i, d)
+            y_copy(i, yy).start()
+
+        @pl.when((i >= 1) & (i < CHUNKS + 1))
+        def _():
+            ch = i - 1
+            y_copy(ch, 1 - yy).wait_recv()
+            c_copy(ch, core).start()
+
+        @pl.when((i >= 2) & (i < CHUNKS + 2))
+        def _():
+            ch = i - 2
+            c_copy(ch, 1 - core).wait_recv()
+            for z in range(nz):
+                for y in range(2):
+                    a = x[ch, 0, y, z].astype(jnp.float32)
+                    b = x[ch, 1, y, z].astype(jnp.float32)
+                    m = 16 * (z * 2 + y)
+                    xf[ch, m:m + 16, :] = jnp.concatenate([a, b], 0).astype(jnp.bfloat16)
+            size = f1.shape[3]
+            for s in range(sub):
+                lacc[...] += lax.dot_general(
+                    f1[kslot, ch * sub + s], xf[ch, :, s * size:(s + 1) * size],
+                    (((1,), (1,)), ((), ())), preferred_element_type=jnp.float32,
+                )
+
+        @pl.when(i == R1_AT)
+        def _():
+            own_p.wait()
+            far_p.wait_recv()
+            for z in range(nz):
+                sbuf[z] = pbuf[pick, z, 1 - yy]
+                ry_copy(z).start()
+                tbuf[z] = pbuf[pick, z, yy]
+
+        @pl.when(i == R2_AT)
+        def _():
+            for z in range(nz):
+                remote(
+                    sbuf.at[z], qbuf.at[1 - yy, z], rys.at[z], ryr.at[z],
+                    at(zz, 1 - yy, core),
+                ).wait_recv()
+                qbuf[yy, z] = tbuf[z]
+            for z in range(nz):
+                tbuf[z] = qbuf[oy, z]
+            for d in range(1, nz):
+                rz_copy(d).start()
+            fbuf[zz] = tbuf[zz]
+
+        @pl.when(i == CHUNKS + 1)
+        def _():
+            lc[core] = lacc[...].astype(jnp.bfloat16)
+            l_core.start()
+
+        @pl.when(i == CHUNKS + 2)
+        def _():
+            l_copy(0, lc.at[core], lc.at[1 - core], at(zz, yy, 1 - core)).wait_recv()
+            ly[yy] = lc[oc]
+            l_y.start()
+
+        @pl.when(i >= 3)
+        def _():
+            ch = i - 3
+            for half, src, acc in ((0, wg, ag), (1, wu, au)):
+                w_copy(src, ch, half).wait()
+                slot_w = lax.rem(ch * 2 + half, SLOTS)
+                for n in range(0, width, 256):
+                    acc[:, n:n + 256] += jnp.dot(
+                        xf[ch], w[slot_w, :, n:n + 256], preferred_element_type=jnp.float32
+                    )
+
+                @pl.when(ch + SLOTS // 2 < CHUNKS)
+                def _():
+                    w_copy(src, ch + SLOTS // 2, half).start()
+
+        return 0
+
+    lax.fori_loop(0, CHUNKS + 3, step, 0)
+
+    l_copy(1, ly.at[yy], ly.at[1 - yy], at(zz, 1 - yy, core)).wait_recv()
+    lz[zz] = ly[oy]
+    for d in range(1, nz):
+        l_z(d).start()
+    for d in range(1, nz):
+        remote(
+            tbuf.at[far(d)], fbuf.at[near(d)], rzs.at[d - 1], rzr.at[d - 1],
+            at(far(d), yy, core),
+        ).wait_recv()
+    for d in range(1, nz):
+        l_copy(1 + d, lz.at[zz], lz.at[near(d)], at(far(d), yy, core)).wait_recv()
+    lstage[...] = lz[oz]
+    rank = lstage.shape[0] // 2
+    dims = (((0,), (0,)), ((), ()))
+    for n in range(0, width, 256):
+        g = ag[:, n:n + 256] + lax.dot_general(
+            lstage[:rank], fbuf[oz, :rank, n:n + 256], dims, preferred_element_type=jnp.float32
+        )
+        u = au[:, n:n + 256] + lax.dot_general(
+            lstage[rank:], fbuf[oz, rank:, n:n + 256], dims, preferred_element_type=jnp.float32
+        )
+        out[:, n:n + 256] = (g / (1.0 + jnp.exp(-g)) * u).astype(out.dtype)
+
+    def drain(ch, _):
+        for d in range(1, nz):
+            z_copy(ch, d).wait_send()
+        y_copy(ch, yy).wait_send()
+        c_copy(ch, core).wait_send()
+        return 0
+
+    lax.fori_loop(0, CHUNKS, drain, 0)
+    far_p.wait_send()
+    for z in range(nz):
+        ry_copy(z).wait_send()
+    for d in range(1, nz):
+        rz_copy(d).wait_send()
+        l_z(d).wait_send()
+    l_core.wait_send()
+    l_y.wait_send()
+
+
+def fused(tensor, tokens, gate_weight, up_weight, first_store, second_store, adapter_ids, owner_map):
+    nz = tensor // 4
+    keep = first_store.shape[0]
+    doubled, width = second_store.shape[2:]
+    depth = tokens.shape[1]
+    kc = depth // CHUNKS
+    rows = tokens.shape[0] * tensor
+    second = second_store.reshape(keep, nz, 2, 2, doubled, width)
+    any_, vmem, smem = (
+        pl.BlockSpec(memory_space=s) for s in (pl.ANY, pltpu.VMEM, pltpu.SMEM)
+    )
+    bf, f32 = jnp.bfloat16, jnp.float32
+    dma = pltpu.SemaphoreType.DMA
+    return pl.pallas_call(
+        functools.partial(kernel, nz, keep),
+        out_shape=jax.ShapeDtypeStruct((rows, width), bf),
+        in_specs=[any_, any_, any_, vmem, any_, smem, smem],
+        out_specs=vmem,
+        scratch_shapes=[
+            pltpu.VMEM((CHUNKS, 2, 2, nz, tokens.shape[0], kc), bf),
+            pltpu.VMEM((CHUNKS, rows, kc), bf),
+            pltpu.VMEM((SLOTS, kc, width), bf),
+            pltpu.VMEM((rows, width), f32),
+            pltpu.VMEM((rows, width), f32),
+            pltpu.VMEM((2 * keep, nz, 2, doubled, width), bf),
+            pltpu.VMEM((nz, doubled, width), bf),
+            pltpu.VMEM((2, nz, doubled, width), bf),
+            pltpu.VMEM((nz, doubled, width), bf),
+            pltpu.VMEM((nz, doubled, width), bf),
+            pltpu.VMEM((doubled, rows), f32),
+            pltpu.VMEM((doubled, rows), bf),
+            pltpu.VMEM((2, doubled, rows), bf),
+            pltpu.VMEM((2, doubled, rows), bf),
+            pltpu.VMEM((nz, doubled, rows), bf),
+            dma((CHUNKS,)), dma((SLOTS,)), dma((1,)),
+            dma((CHUNKS, nz - 1)), dma((CHUNKS, nz - 1)),
+            dma((CHUNKS,)), dma((CHUNKS,)), dma((CHUNKS,)), dma((CHUNKS,)),
+            dma((1,)), dma((1,)), dma((nz,)), dma((nz,)), dma((nz - 1,)), dma((nz - 1,)),
+            dma((nz + 1,)), dma((nz + 1,)),
+        ],
+        compiler_params=pltpu.CompilerParams(
+            collective_id=0, has_side_effects=True, vmem_limit_bytes=63 * 1024 * 1024
+        ),
+        cost_estimate=pl.CostEstimate(
+            flops=4 * rows * depth * width, bytes_accessed=4 * depth * width,
+            transcendentals=rows * width,
+        ),
+    )(tokens, gate_weight, up_weight, first_store, second, adapter_ids, owner_map)
+
+
 def solution(mesh):
+    tensor = mesh.shape["tensor"]
+
+    def per_device(*args):
+        if tensor == 16 and args[5].shape[0] == 1:
+            return fused(tensor, *args)
+        return general(*args)
+
     placed = (
         P(("groups", "tensor"), None),
         P(None, "tensor"),

time: 239 us -> 58.9 us (0.25)
  waiting for transfers between devices: 154 us -> 0 us
  Pallas kernels: 0 us -> 56.2 us
  matrix products: 30.6 us -> 0 us
  blocking collectives: 21 us -> 0 us
  between operations: 18.1 us -> 0.66 us
  starting transfers between devices: 7.64 us -> 0 us
  other arithmetic: 2.53 us -> 0 us
  local copies, waits for them, and re-layouts: 4.34 us -> 1.82 us
    psum x1 -> x0, waiting for transfers between devices: 133 us -> none  [spread(): return lax.psum(jnp.where(mine, value, jnp.zeros_like(value)), axis)]
    pallas_call x0 -> x1, Pallas kernels: none -> 56.2 us  [fused(): pl.pallas_call(functools.partial(kernel, nz, keep), out_shape=jax.ShapeDt...]
    dot_general x4 -> x0, matrix products: 30.6 us -> none  [the longest x1 14.8 us: per_device(): jnp.dot(whole, gate_weight, preferred_element_type=jnp.float32) + delta[0]]
    all_gather x1 -> x0, blocking collectives: 21 us -> none  [per_device(): lax.all_gather(lowrank, 'tensor', axis=0, tiled=True)]
    all_gather x1 -> x0, waiting for transfers between devices: 20.3 us -> none  [per_device(): lax.all_gather(tokens, 'tensor', axis=0, tiled=True)]
    all_to_all x1 -> x0, starting transfers between devices: 7.56 us -> none  [per_device(): lax.all_to_all(second_store, 'tensor', split_axis=1, concat_axis=0, tiled...]
    unnamed x9 -> x1, local copies, waits for them, and re-layouts: 4.21 us -> 1.82 us
  transfers between devices with their start and end apart: 3 -> 0, of which waited for: 2 -> 0; matrix products, arithmetic and copies ran while one was open for 2% -> 0% of each run, Pallas kernels for 0% -> 0%
where the time goes in v1:
time: 58.9 us; the launch traced here: 58.7 us
  Pallas kernels  56.2 us (95%)
  local copies, waits for them, and re-layouts  1.82 us (3%)
  between operations  0.66 us (1%)
    pallas_call x1, Pallas kernels, fused(): pl.pallas_call(functools.partial(kernel, nz, keep), out_shape=jax.ShapeDt...  56.2 us
    unnamed x1, local copies, waits for them, and re-layouts  1.82 us

profile of v1, /device:TPU:0, one launch (start us, length us, event | category | flops | bytes accessed | tf_op | source)
XLA Modules:
  0.0 58.7 jit_solution(13036080762045427401)
XLA Ops:
  0.7 56.2 %shard_map.73 = bf16[128,1792]{1,0:T(8,128)(2,1)} custom-call(bf16[8,8192]{1,0:T(8,128)(2,1)} %tok.1, bf16[8192,1792]{1,0:T(8,128)(2,1)} %wg.1, bf16[8192,1792]{1,0:T(8,128)(2,1)} %wu.1, bf16[2,16,32,512]{3,2,1,0:T(8,128)(2,1)} %f1.1, bf16[2,4,2,2,32,1792]{5,4,3,2,1,0:T(8,128)(2,1)} %bitcast.1, s32[1]{0:T(128)S(6)} %copy.9.ids, s32[32]{0:T(128)} %omap.1), custom_call_target="tpu_custom_call" | custom-call | flops 7516192768 | bytes 58720256 | tf_op jit(solution)/shard_map/pallas_call | solution.py:320
  56.9 1.8 %copy.10 = bf16[128,1792]{1,0:T(8,128)(2,1)} copy(bf16[128,1792]{1,0:T(8,128)(2,1)} %shard_map.73) | data formatting | bytes 917504

commit v2 on v1

--- a/solution.py
+++ b/solution.py
@@ -7,9 +7,9 @@
 from jax.sharding import PartitionSpec as P
 
 PLEN = 128
-CHUNKS = 8
-SLOTS = 12
-R1_AT, R2_AT = 4, 9
+CHUNKS = 4
+SLOTS = 6
+R1_AT, R2_AT = 2, (6, 4, 5, 6)
 MESH = pl.DeviceIdType.MESH
 
 
@@ -214,24 +214,25 @@
         def _():
             own_p.wait()
             far_p.wait_recv()
-            for z in range(nz):
+            for d in (*range(1, nz), 0):
+                z = far(d)
                 sbuf[z] = pbuf[pick, z, 1 - yy]
                 ry_copy(z).start()
-                tbuf[z] = pbuf[pick, z, yy]
-
-        @pl.when(i == R2_AT)
-        def _():
-            for z in range(nz):
+                qbuf[yy, z] = pbuf[pick, z, yy]
+
+        for d in (*range(1, nz), 0):
+            @pl.when(i == R2_AT[d])
+            def _():
+                z = far(d)
                 remote(
                     sbuf.at[z], qbuf.at[1 - yy, z], rys.at[z], ryr.at[z],
                     at(zz, 1 - yy, core),
                 ).wait_recv()
-                qbuf[yy, z] = tbuf[z]
-            for z in range(nz):
-                tbuf[z] = qbuf[oy, z]
-            for d in range(1, nz):
-                rz_copy(d).start()
-            fbuf[zz] = tbuf[zz]
+                tbuf[z] = jnp.where(oy == yy, qbuf[yy, z], qbuf[1 - yy, z])
+                if d:
+                    rz_copy(d).start()
+                else:
+                    fbuf[zz] = tbuf[zz]
 
         @pl.when(i == CHUNKS + 1)
         def _():

time: 58.9 us -> 52.7 us (0.89)
  Pallas kernels: 56.2 us -> 50.1 us
    pallas_call x1, Pallas kernels: 56.2 us -> 50.1 us  [fused(): pl.pallas_call(functools.partial(kernel, nz, keep), out_shape=jax.ShapeDt...]
where the time goes in v2:
time: 52.7 us; the launch traced here: 52.5 us
  Pallas kernels  50.1 us (95%)
  local copies, waits for them, and re-layouts  1.82 us (3%)
  between operations  0.66 us (1%)
    pallas_call x1, Pallas kernels, fused(): pl.pallas_call(functools.partial(kernel, nz, keep), out_shape=jax.ShapeDt...  50.1 us
    unnamed x1, local copies, waits for them, and re-layouts  1.82 us

profile of v2, /device:TPU:0, one launch (start us, length us, event | category | flops | bytes accessed | tf_op | source)
XLA Modules:
  0.0 52.5 jit_solution(9695883670730390725)
XLA Ops:
  0.7 50.1 %shard_map.73 = bf16[128,1792]{1,0:T(8,128)(2,1)} custom-call(bf16[8,8192]{1,0:T(8,128)(2,1)} %tok.1, bf16[8192,1792]{1,0:T(8,128)(2,1)} %wg.1, bf16[8192,1792]{1,0:T(8,128)(2,1)} %wu.1, bf16[2,16,32,512]{3,2,1,0:T(8,128)(2,1)} %f1.1, bf16[2,4,2,2,32,1792]{5,4,3,2,1,0:T(8,128)(2,1)} %bitcast.1, s32[1]{0:T(128)S(6)} %copy.9.ids, s32[32]{0:T(128)} %omap.1), custom_call_target="tpu_custom_call" | custom-call | flops 7516192768 | bytes 58720256 | tf_op jit(solution)/shard_map/pallas_call | solution.py:321
  50.7 1.8 %copy.10 = bf16[128,1792]{1,0:T(8,128)(2,1)} copy(bf16[128,1792]{1,0:T(8,128)(2,1)} %shard_map.73) | data formatting | bytes 917504

commit v3 on v2

--- a/solution.py
+++ b/solution.py
@@ -9,7 +9,7 @@
 PLEN = 128
 CHUNKS = 4
 SLOTS = 6
-R1_AT, R2_AT = 2, (6, 4, 5, 6)
+R1_AT, R2_AT = 3, (6, 5, 6, 6)
 MESH = pl.DeviceIdType.MESH
 
 

time: 52.7 us -> 47.7 us (0.905)
  Pallas kernels: 50.1 us -> 45.1 us
    pallas_call x1, Pallas kernels: 50.1 us -> 45.1 us  [fused(): pl.pallas_call(functools.partial(kernel, nz, keep), out_shape=jax.ShapeDt...]
where the time goes in v3:
time: 47.7 us; the launch traced here: 47.6 us
  Pallas kernels  45.1 us (95%)
  local copies, waits for them, and re-layouts  1.82 us (4%)
  between operations  0.66 us (1%)
    pallas_call x1, Pallas kernels, fused(): pl.pallas_call(functools.partial(kernel, nz, keep), out_shape=jax.ShapeDt...  45.1 us
    unnamed x1, local copies, waits for them, and re-layouts  1.82 us

profile of v3, /device:TPU:0, one launch (start us, length us, event | category | flops | bytes accessed | tf_op | source)
XLA Modules:
  0.0 47.6 jit_solution(3468539637348992773)
XLA Ops:
  0.7 45.1 %shard_map.73 = bf16[128,1792]{1,0:T(8,128)(2,1)} custom-call(bf16[8,8192]{1,0:T(8,128)(2,1)} %tok.1, bf16[8192,1792]{1,0:T(8,128)(2,1)} %wg.1, bf16[8192,1792]{1,0:T(8,128)(2,1)} %wu.1, bf16[2,16,32,512]{3,2,1,0:T(8,128)(2,1)} %f1.1, bf16[2,4,2,2,32,1792]{5,4,3,2,1,0:T(8,128)(2,1)} %bitcast.1, s32[1]{0:T(128)S(6)} %copy.9.ids, s32[32]{0:T(128)} %omap.1), custom_call_target="tpu_custom_call" | custom-call | flops 7516192768 | bytes 58720256 | tf_op jit(solution)/shard_map/pallas_call | solution.py:321
  45.7 1.8 %copy.10 = bf16[128,1792]{1,0:T(8,128)(2,1)} copy(bf16[128,1792]{1,0:T(8,128)(2,1)} %shard_map.73) | data formatting | bytes 917504
